TPU v7x, 32 devices: a whole 2x2x4 slice. The times are simulated.
32 devices in a mesh: row: 8 (over y, x, core), col: 4 (over z).
Axes of the slice: x: 2, y: 2, z: 4, core: 2. Of those that a mesh axis runs over, the one named last changes fastest.
Arguments:
- stored_blocks: float32 [256, 8, 128, 128], P('row', 'col'), may hold values from -1.8 to 1.8
- block_cols: int32 [256, 8], P('row', 'col'), may hold values from 0 to 31, as said below
- storage_map: int32 [256, 8], P('row', 'col'), may hold values from 0 to 1, as said below
Outputs:
- square_part: float32 [256, 8, 128, 128], P('row', 'col')
Inputs may be any that keep to these rules, and one draw needn't show every extreme that they name: The block pattern is symmetric: block (R, q) with column C = q * 32 + block_cols[R, q] has block_cols[C, R // 32] == R mod 32; every slab pairs its block rows with its block columns one to one; block_cols[R, R // 32] == R mod 32. Of a block and its mirror image exactly one has storage_map 1; blocks on the diagonal have 1.
All inputs are finite; a program needn't handle non-finite values.
Results may differ from a plain program's by a relative error of at most 0.0001.
Values sent between devices are 32-bit elements; how exact they have to be, the bound alone decides.
A program may use at most 128 MiB of HBM per device.

v0:
```python
import jax
import jax.numpy as jnp
from jax import lax
from jax.sharding import PartitionSpec as P

STEPS = 4


def from_root(block, axis, holder):
    block = jnp.where(lax.axis_index(axis) == holder, block, jnp.zeros_like(block))
    return lax.psum(block, axis)


def shifted(block, axis, distance):
    devices = range(lax.axis_size(axis))
    route = [((i - distance) % len(devices), i) for i in devices]
    return lax.ppermute(block, axis, route)


def mirror_columns(masked):
    first = lax.all_to_all(masked, "col", split_axis=0, concat_axis=1, tiled=True)
    return lax.all_to_all(
        lax.all_to_all(first, "row", split_axis=1, concat_axis=1, tiled=True),
        "col",
        split_axis=1,
        concat_axis=0,
        tiled=True,
    )


def shards(stored_blocks, block_cols, storage_map):
    rows_total, groups = block_cols.shape
    row_count = lax.axis_size("row")
    masked = stored_blocks * storage_map.astype(jnp.float32)[:, :, None, None]
    arrived = mirror_columns(masked)
    group_ids = jnp.arange(groups, dtype=jnp.int32)[None, :]
    mirrored = arrived[block_cols, group_ids]
    density = masked + jnp.swapaxes(mirrored, 2, 3)
    col_float = block_cols.astype(jnp.float32)
    row_index = lax.axis_index("row")
    total = jnp.zeros(density.shape, jnp.float32)
    panel, panel_cols = (density, col_float)
    for step in range(STEPS):
        kappa = (row_index + step) % row_count
        holder = kappa // groups
        within = kappa % groups
        left_piece = lax.dynamic_index_in_dim(density, within, 1, keepdims=False)
        left_cols = lax.dynamic_index_in_dim(col_float, within, 1, keepdims=False)
        left_vals, left_colf = (
            from_root(left_piece, "col", holder),
            from_root(left_cols, "col", holder),
        )
        if step > 0:
            panel, panel_cols = shifted((panel, panel_cols), "row", -1)
        inner = left_colf.astype(jnp.int32)
        right = panel[inner]
        match = panel_cols[inner].astype(jnp.int32) == block_cols
        term = jnp.einsum("rik,rukj->ruij", left_vals, right, precision=lax.Precision.HIGHEST)
        total = total + jnp.where(match[:, :, None, None], term, jnp.float32(0.0))
    return total


def solution(mesh):
    return jax.shard_map(
        shards,
        mesh=mesh,
        in_specs=(P("row", "col", None, None), P("row", "col"), P("row", "col")),
        out_specs=P("row", "col", None, None),
        check_vma=False,
    )
```

profile of v0, /device:TPU:25, one launch (start us, length us, event | category | flops | bytes accessed | tf_op | source)
XLA Modules:
  0.0 643.5 jit_solution(5802590032220360528)
XLA Ops:
  6.5 0.7 convert_element_type.33
  7.2 2.5 copy_multiply_fusion
  9.7 0.5 copy.84
  10.2 95.5 %all_to_all.41 = f32[32,2,128,128]{3,2,1,0:T(8,128)S(1)} all-to-all(f32[32,2,128,128]{3,2,1,0:T(8,128)S(1)} %copy.84), channel_id=1, replica_groups=mesh['row'=8,'col'=4] {'col'}, dimensions={0} | all-to-all | bytes 8388608 | tf_op jit(solution)/shard_map/all_to_all | solution.py:21
  105.7 0.5 copy.85
  106.2 0.5 copy.86
  106.7 52.5 %all_to_all.42 = f32[8,8,128,128]{3,2,0,1:T(8,128)} all-to-all(f32[8,8,128,128]{3,2,0,1:T(8,128)S(1)} %copy.86), channel_id=1, replica_groups=mesh['row'=8,'col'=4] {'row'}, dimensions={1} | all-to-all | bytes 8388608 | tf_op jit(solution)/shard_map/all_to_all | solution.py:23
  159.2 0.0 copy-start.4
  159.2 6.7 %all-to-all-start.2 = ((f32[8,8,128,128]{3,2,0,1:T(8,128)}), f32[8,8,128,128]{3,2,0,1:T(8,128)}, u32[]{:S(2)}, u32[]{:S(2)}) async-start(f32[8,8,128,128]{3,2,0,1:T(8,128)} %all_to_all.42), calls=%async_computation.2 | async-start | bytes 8388608 | tf_op jit(solution)/shard_map/all_to_all | solution.py:22
  166.0 0.0 all-reduce.4.cloned.1.call-start
  166.0 0.0 copy-done.4
  166.0 0.1 copy.89
  166.1 0.1 reshape.40
  166.2 89.7 %all-to-all-done.2 = f32[8,8,128,128]{3,2,0,1:T(8,128)} async-done(((f32[8,8,128,128]{3,2,0,1:T(8,128)}), f32[8,8,128,128]{3,2,0,1:T(8,128)}, u32[]{:S(2)}, u32[]{:S(2)}) %all-to-all-start.2) | async-done | bytes 4194336 | tf_op jit(solution)/shard_map/all_to_all | solution.py:22
  255.8 4.7 copy.88
  260.5 4.9 gather_fusion.1
  265.5 5.6 copy.90
  271.1 5.9 bitcast_add_fusion
  277.0 2.2 collective-permute-start.1
  279.2 7.4 %select_bitcast_fusion = (f32[32,128,128]{2,1,0:T(8,128)}, f32[32,128,128]{2,1,0:T(8,128)}, f32[32,128,128]{2,1,0:T(8,128)}, f32[32,128,128]{2,1,0:T(8,128)}) fusion(f32[32,2,128,128]{3,2,0,1:T(8,128)} %bitcast_add_fusion, s32[]{:T(128)S(6)} %select_n.220, pred[]{:T(512)S(6)} %eq.43, s32[]{:T(128)S(6)} %select_n.208, pred[]{:T(512)S(6)} %eq.41, ...), kind=kLoop, calls=%fused_computation.19 | loop fusion | flops 2097152 | bytes 16777236 | tf_op jit(solution)/shard_map/jit(_where)/select_n | solution.py:10
  286.7 0.0 all-reduce.4.cloned.1.call-update
  286.7 40.3 %collective-permute-done.1 = f32[32,2,128,128]{3,2,0,1:T(8,128)} collective-permute-done((f32[32,2,128,128]{3,2,0,1:T(8,128)}, f32[32,2,128,128]{3,2,0,1:T(8,128)}, u32[]{:S(2)}, u32[]{:S(2)}) %collective-permute-start.1) | collective-permute-done | bytes 4194336 | tf_op jit(solution)/shard_map/ppermute | solution.py:17
  327.0 0.0 collective-permute-start.3
  327.0 48.5 %collective-permute-done.3 = f32[32,2,128,128]{3,2,0,1:T(8,128)} collective-permute-done((f32[32,2,128,128]{3,2,0,1:T(8,128)}, f32[32,2,128,128]{3,2,0,1:T(8,128)}, u32[]{:S(2)}, u32[]{:S(2)}) %collective-permute-start.3) | collective-permute-done | bytes 4194336 | tf_op jit(solution)/shard_map/ppermute | solution.py:17
  375.5 0.0 collective-permute-start.5
  375.5 0.1 copy.80
  375.6 2.6 collective-permute-start
  378.2 0.2 select_reduce_fusion
  378.5 8.1 %all-reduce = (f32[32]{0:T(128)S(1)}, f32[32]{0:T(128)S(1)}, f32[32]{0:T(128)S(1)}, f32[32]{0:T(128)S(1)}) all-reduce(f32[32]{0:T(128)S(1)} %get-tuple-element.6, f32[32]{0:T(128)S(1)} %get-tuple-element.7, f32[32]{0:T(128)S(1)} %get-tuple-element.8, f32[32]{0:T(128)S(1)} %get-tuple-element.5), channel_id=1, replica_groups=mesh['row'=8,'col'=4] {'col'}, use_global_device_ids=true, to_apply=%region_4.5 | all-reduce | flops 128 | bytes 1024 | tf_op jit(solution)/shard_map/psum | solution.py:11
  386.6 37.6 %collective-permute-done = f32[32,2]{1,0:T(8,128)S(1)} collective-permute-done((f32[32,2]{1,0:T(8,128)S(1)}, f32[32,2]{1,0:T(8,128)S(1)}, u32[]{:S(2)}, u32[]{:S(2)}) %collective-permute-start) | collective-permute-done | bytes 288 | tf_op jit(solution)/shard_map/ppermute | solution.py:17
  424.2 0.3 collective-permute-start.2
  424.5 0.6 gather_fusion
  425.1 2.7 collective-permute-done.2
  427.8 1.4 collective-permute-start.4
  429.2 0.1 copy.81
  429.3 0.6 gather_fusion.3
  429.8 0.1 copy.92
  429.9 0.6 gather_fusion.5
  430.5 0.1 copy.95
  430.6 0.4 collective-permute-done.4
  430.9 0.6 gather_fusion.7
  431.5 0.1 copy.98
  431.6 0.1 copy.82
  431.7 0.1 copy.93
  431.8 0.1 copy.99
  431.9 0.1 copy.96
  432.0 4.9 gather_fusion.2
  437.0 5.3 gather_fusion.4
  442.2 135.1 %all-reduce.4.cloned.1.call-done = (f32[32,128,128]{2,1,0:T(8,128)}, f32[32,128,128]{2,1,0:T(8,128)}, f32[32,128,128]{2,1,0:T(8,128)}, f32[32,128,128]{2,1,0:T(8,128)}) async-done(((f32[32,128,128]{2,1,0:T(8,128)}, f32[32,128,128]{2,1,0:T(8,128)}, f32[32,128,128]{2,1,0:T(8,128)}, f32[32,128,128]{2,1,0:T(8,128)}), (f32[32,128,128]{2,1,0:T(8,128)}, f32[32,128,128]{2,1,0:T(8,128)}, f32[32,128,128]{2,1,0:T(8,128)}, ...) | async-done | bytes 8388624 | tf_op jit(solution)/shard_map/psum | solution.py:11
  577.3 0.0 copy-start.3
  577.3 10.7 %fusion.5 = f32[32,2,128,128]{3,2,1,0:T(8,128)} fusion(f32[32,2,128,128]{3,2,1,0:T(8,128)} %gather_fusion.2, f32[32,128,128]{2,1,0:T(8,128)} %get-tuple-element.15), kind=kOutput, calls=%fused_computation.17 | convolution fusion | flops 1610612736 | bytes 10485760 | tf_op jit(solution)/shard_map/rik,rukj->ruij/dot_general | solution.py:58
  588.1 0.0 copy-done
  588.1 0.0 copy-done.3
  588.1 8.9 %fusion.3 = f32[32,2,128,128]{3,2,1,0:T(8,128)} fusion(f32[32,2,128,128]{3,2,1,0:T(8,128)S(1)} %copy-done, f32[32,128,128]{2,1,0:T(8,128)S(1)} %copy-done.3), kind=kOutput, calls=%fused_computation.15 | convolution fusion | flops 1610612736 | bytes 10485760 | tf_op jit(solution)/shard_map/rik,rukj->ruij/dot_general | solution.py:58
  596.9 0.0 copy-start.2
  596.9 5.2 gather_fusion.6
  602.1 0.0 copy-done.2
  602.1 10.4 %fusion.1 = f32[32,2,128,128]{3,2,1,0:T(8,128)} fusion(f32[32,2,128,128]{3,2,1,0:T(8,128)} %gather_fusion.6, f32[32,128,128]{2,1,0:T(8,128)S(1)} %copy-done.2), kind=kOutput, calls=%fused_computation.13 | convolution fusion | flops 1610612736 | bytes 10485760 | tf_op jit(solution)/shard_map/rik,rukj->ruij/dot_general | solution.py:58
  612.5 0.0 copy-start.1
  612.5 0.0 collective-permute-done.5
  612.5 5.2 gather_fusion.8
  617.7 0.0 copy-done.1
  617.7 13.4 %add_bitcast_fusion = f32[32,2,128,128]{2,3,1,0:T(8,128)} fusion(f32[32,2,128,128]{3,2,1,0:T(8,128)} %fusion.1, f32[32,2,128,128]{3,2,1,0:T(8,128)} %fusion.3, f32[32,2,128,128]{3,2,1,0:T(8,128)} %fusion.5, f32[32,2,128,128]{3,2,1,0:T(8,128)} %gather_fusion.8, f32[32,128,128]{2,1,0:T(8,128)S(1)} %copy-done.1, pred[32,2]{1,0:T(8,128)(4,1)S(1)} %copy.99, ...), kind=kOutput, calls=%fused_computation.11 | convolution fusion | flops 1617952768 | bytes 23068928 | tf_op jit(solution)/shard_map/rik,rukj->ruij/dot_general | solution.py:58
  631.1 5.6 copy.101
  (12 shorter events, 0.1 us)
Async XLA Ops:
  159.2 6.7 %copy-start.4 = (s32[32,2]{0,1:T(2,128)S(1)}, s32[32,2]{0,1:T(2,128)}, u32[]{:S(2)}) copy-start(s32[32,2]{0,1:T(2,128)} %param.4) | copy-start | bytes 772
  159.2 96.6 %all-to-all-start.2 = ((f32[8,8,128,128]{3,2,0,1:T(8,128)}), f32[8,8,128,128]{3,2,0,1:T(8,128)}, u32[]{:S(2)}, u32[]{:S(2)}) async-start(f32[8,8,128,128]{3,2,0,1:T(8,128)} %all_to_all.42), calls=%async_computation.2 | async-start | bytes 8388608 | tf_op jit(solution)/shard_map/all_to_all | solution.py:22
  166.0 411.4 %all-reduce.4.cloned.1.call-start = ((), (), s32[]{:S(2)}) async-start(), calls=%async_computation.3 | async-start | bytes 16777216 | tf_op jit(solution)/shard_map/psum | solution.py:11
  277.0 50.0 %collective-permute-start.1 = (f32[32,2,128,128]{3,2,0,1:T(8,128)}, f32[32,2,128,128]{3,2,0,1:T(8,128)}, u32[]{:S(2)}, u32[]{:S(2)}) collective-permute-start(f32[32,2,128,128]{3,2,0,1:T(8,128)} %bitcast_add_fusion), channel_id=1, source_target_pairs={{4,0},{8,4},{12,8},{16,12},{20,16},{24,20},{28,24},{0,28},{5,1},{9... | collective-permute-start | bytes 12582920 | tf_op jit(solution)/shard_map/ppermute | solution.py:17
  327.0 48.5 %collective-permute-start.3 = (f32[32,2,128,128]{3,2,0,1:T(8,128)}, f32[32,2,128,128]{3,2,0,1:T(8,128)}, u32[]{:S(2)}, u32[]{:S(2)}) collective-permute-start(f32[32,2,128,128]{3,2,0,1:T(8,128)} %collective-permute-done.1), channel_id=1, source_target_pairs={{4,0},{8,4},{12,8},{16,12},{20,16},{24,20},{28,24},{0,28},{5,1},{9... | collective-permute-start | bytes 12582920 | tf_op jit(solution)/shard_map/ppermute | solution.py:17
  375.5 237.0 %collective-permute-start.5 = (f32[32,2,128,128]{3,2,0,1:T(8,128)}, f32[32,2,128,128]{3,2,0,1:T(8,128)}, u32[]{:S(2)}, u32[]{:S(2)}) collective-permute-start(f32[32,2,128,128]{3,2,0,1:T(8,128)} %collective-permute-done.3), channel_id=1, source_target_pairs={{4,0},{8,4},{12,8},{16,12},{20,16},{24,20},{28,24},{0,28},{5,1},{9... | collective-permute-start | bytes 12582920 | tf_op jit(solution)/shard_map/ppermute | solution.py:17
  375.6 48.6 %collective-permute-start = (f32[32,2]{1,0:T(8,128)S(1)}, f32[32,2]{1,0:T(8,128)S(1)}, u32[]{:S(2)}, u32[]{:S(2)}) collective-permute-start(f32[32,2]{1,0:T(8,128)S(1)} %convert_element_type.30), channel_id=1, source_target_pairs={{4,0},{8,4},{12,8},{16,12},{20,16},{24,20},{28,24},{0,28},{5,1},{9... | collective-permute-start | bytes 776 | tf_op jit(solution)/shard_map/ppermute | solution.py:17
  424.2 3.6 collective-permute-start.2
  427.8 3.2 collective-permute-start.4
  577.3 10.7 %copy-start = (f32[32,2,128,128]{3,2,1,0:T(8,128)S(1)}, f32[32,2,128,128]{3,2,1,0:T(8,128)}, u32[]{:S(2)}) copy-start(f32[32,2,128,128]{3,2,1,0:T(8,128)} %gather_fusion.4) | copy-start | bytes 12582916
  577.3 10.7 %copy-start.3 = (f32[32,128,128]{2,1,0:T(8,128)S(1)}, f32[32,128,128]{2,1,0:T(8,128)}, u32[]{:S(2)}) copy-start(f32[32,128,128]{2,1,0:T(8,128)} %get-tuple-element.14) | copy-start | bytes 6291460
  596.9 5.2 copy-start.2
  612.5 5.2 copy-start.1
Sparse Core Ops, SparseCore 0:
  286.8 290.4 all-reduce.3
where the time goes:
time: 648 us; the launch traced here: 644 us
  waiting for transfers between devices  354 us (55%)
  blocking collectives  156 us (24%)
  local copies, waits for them, and re-layouts  46.1 us (7%)
  matrix products  43.4 us (7%)
  other arithmetic  16.9 us (3%)
  between operations  13.5 us (2%)
  starting transfers between devices  13.4 us (2%)
    psum x1, waiting for transfers between devices, from_root(): return lax.psum(block, axis)  135 us
    ppermute x6, waiting for transfers between devices, shifted(): return lax.ppermute(block, axis, route)  129 us
    all_to_all x1, blocking collectives, mirror_columns(): lax.all_to_all(masked, 'col', split_axis=0, concat_axis=1, tiled=True)  95.5 us
    all_to_all x1, waiting for transfers between devices, mirror_columns(): lax.all_to_all(lax.all_to_all(first, 'row', split_axis=1, concat_axis=1,...  89.7 us
    all_to_all x1, blocking collectives, mirror_columns(): lax.all_to_all(first, 'row', split_axis=1, concat_axis=1, tiled=True)  52.5 us
    dot_general x4, matrix products, shards(): jnp.einsum('rik,rukj->ruij', left_vals, right, precision=lax.Precision.HI...  43.4 us
    gather x4, local copies, waits for them, and re-layouts, shards(): right = panel[inner]  20.5 us
  transfers between devices with their start and end apart: 8, of which 7 were waited for; matrix products, arithmetic and copies ran while one was open for 9% of the time, Pallas kernels for 0%

commit v1 on v0

v1 whole, which is shorter than its diff:
```python
import functools

import jax
import jax.numpy as jnp
from jax import lax
from jax.experimental import pallas as pl
from jax.experimental.pallas import tpu as pltpu
from jax.sharding import PartitionSpec as P

STEPS = 4
CHUNKS = 4
MESH = pl.DeviceIdType.MESH


def kernel(n_row, n_col, x_ref, cols_ref, map_ref, out_ref, arr, relay, dens, panels, lefts,
           dir_s, dir_r, rel_s, rel_r, fwd_s, last_s, last_r, self_s,
           pan_s, pan_r, own_s, left_s, left_r):
    blk, groups = x_ref.shape[0], x_ref.shape[1]
    bs = x_ref.shape[2]
    slabs = n_row
    half = blk // 2
    part = blk // CHUNKS
    r, c = lax.axis_index("row"), lax.axis_index("col")
    home, slot = r // groups, r % groups
    core = r % 2

    def remote(src, dst, ss, rs, row, col):
        return pltpu.make_async_remote_copy(
            src_ref=src, dst_ref=dst, send_sem=ss, recv_sem=rs, device_id=(row, col), device_id_type=MESH)

    barrier = pltpu.get_barrier_semaphore()

    @pl.loop(1, n_col)
    def _(d):
        pl.semaphore_signal(barrier, inc=1, device_id=(r, (c + d) % n_col), device_id_type=MESH)

    @pl.loop(1, n_row)
    def _(d):
        pl.semaphore_signal(barrier, inc=1, device_id=((r + d) % n_row, c), device_id_type=MESH)

    @pl.when(home != c)
    def _():
        for g in range(groups):
            pl.semaphore_signal(barrier, inc=1, device_id=(c * groups + g, home), device_id_type=MESH)
        pl.semaphore_wait(barrier, n_col + n_row - 2 + groups)

    @pl.when(home == c)
    def _():
        pl.semaphore_wait(barrier, n_col + n_row - 2)

    lo, hi = pl.ds(0, half), pl.ds(half, half)

    def land(copy, *place):
        for sl in range(groups):
            @pl.when(slot == sl)
            def _(sl=sl):
                copy(*place, arr[sl]).start()

    def direct(g, tile=arr[0]):
        return remote(x_ref.at[lo, g], tile.at[lo], dir_s.at[g], dir_r.at[slot], c * groups + g, home)

    def to_relay(g):
        return remote(x_ref.at[hi, g], relay.at[c, g], rel_s.at[g], rel_r.at[c, g], r, home)

    def last(g, tile=arr[0]):
        return remote(x_ref.at[hi, g], tile.at[hi], rel_s.at[g], last_r.at[slot], c * groups + g, home)

    def forward(c2, g, tile=arr[0]):
        return remote(relay.at[c2, g], tile.at[hi], fwd_s.at[c2, g], last_r.at[slot], c2 * groups + g, c)

    def own(g):
        return pltpu.make_async_copy(x_ref.at[:, g], arr[g], self_s)

    for g in range(groups):
        @pl.when(home != c)
        def _(g=g):
            to_relay(g).start()

        @pl.when((home == c) & (c * groups + g != r))
        def _(g=g):
            land(last, g)

        @pl.when(c * groups + g != r)
        def _(g=g):
            land(direct, g)

        @pl.when(c * groups + g == r)
        def _(g=g):
            own(g).start()

    @pl.when(home == c)
    def _():
        @pl.loop(1, n_col)
        def _(d):
            c2 = (c + d) % n_col
            for g in range(groups):
                pltpu.make_async_copy(relay.at[c2, g], relay.at[c2, g], rel_r.at[c2, g]).wait()
                land(forward, c2, g)

    def recv(ref, sem):
        pltpu.make_async_copy(ref, ref, sem).wait()

    def panel_two(g):
        return remote(dens.at[:, g], panels.at[1, :, g], pan_s.at[0, g], pan_r.at[1, g], (r + n_row - 2) % n_row, c)

    def panel_sib(g):
        return remote(dens.at[:, g], panels.at[0, :, g], pan_s.at[1, g], pan_r.at[0, g], (r + n_row - 1) % n_row, c)

    def panel_far(g):
        return remote(dens.at[:, g], panels.at[2, :, g], pan_s.at[1, g], pan_r.at[2, g], (r + n_row - 3) % n_row, c)

    def pass_on(g, s):
        return remote(panels.at[1, :, g], panels.at[s, :, g], pan_s.at[2, g], pan_r.at[s, g], r + 1 - 2 * core, c)

    def kappa(s):
        return (r + s) % n_row

    def left_from(s, ch, src, side):
        return remote(src, lefts.at[s, pl.ds(ch * part, part)], left_s.at[s, ch, side], left_r.at[s, ch],
                      r, c + 1 - 2 * side)

    def own_left(s):
        return pltpu.make_async_copy(dens.at[:, kappa(s) % groups], lefts.at[s], own_s.at[s])

    row0 = r * blk
    for g in range(groups):
        q = c * groups + g

        @pl.when(q == r)
        def _(g=g):
            own(g).wait()

        @pl.when(q != r)
        def _(g=g):
            recv(arr[g].at[lo], dir_r.at[g])
            recv(arr[g].at[hi], last_r.at[g])

        on_diag = jnp.where(q == r, 1, 0)

        @pl.loop(0, blk)
        def _(i, g=g, q=q, on_diag=on_diag):
            there = cols_ref[(row0 + i) * slabs + q]
            here = map_ref[i * groups + g]
            same = on_diag * jnp.where(there == i, 1, 0)
            mine = here.astype(jnp.float32)
            other = (1 - here + here * same).astype(jnp.float32)
            dens[i, g] = x_ref[i, g] * mine + arr[g][there].T * other

        for s in range(STEPS):
            @pl.when(kappa(s) == q)
            def _(s=s, g=g):
                for ch in range(CHUNKS):
                    src = dens.at[pl.ds(ch * part, part), g]

                    @pl.when(c + 1 < n_col)
                    def _(src=src, ch=ch, s=s):
                        left_from(s, ch, src, 0).start()

                    @pl.when(c > 0)
                    def _(src=src, ch=ch, s=s):
                        left_from(s, ch, src, 1).start()
                own_left(s).start()

        panel_two(g).start()

        @pl.when(core == 1)
        def _(g=g):
            panel_sib(g).start()

        @pl.when(core == 0)
        def _(g=g):
            panel_far(g).start()

    @pl.loop(1, n_col)
    def _(d):
        for s in range(STEPS):
            h = kappa(s) // groups

            @pl.when(h + d == c)
            def _(s=s):
                for ch in range(CHUNKS):
                    piece = lefts.at[s, pl.ds(ch * part, part)]
                    recv(piece, left_r.at[s, ch])

                    @pl.when(c + 1 < n_col)
                    def _(s=s, ch=ch, piece=piece):
                        left_from(s, ch, piece, 0).start()

            @pl.when(c + d == h)
            def _(s=s):
                for ch in range(CHUNKS):
                    piece = lefts.at[s, pl.ds(ch * part, part)]
                    recv(piece, left_r.at[s, ch])

                    @pl.when(c > 0)
                    def _(s=s, ch=ch, piece=piece):
                        left_from(s, ch, piece, 1).start()

    for g in range(groups):
        recv(panels.at[1, :, g], pan_r.at[1, g])

        @pl.when(core == 0)
        def _(g=g):
            pass_on(g, 0).start()

        @pl.when(core == 1)
        def _(g=g):
            pass_on(g, 2).start()

    for s in range(STEPS):
        @pl.when(kappa(s) // groups == c)
        def _(s=s):
            own_left(s).wait()

    for g in range(groups):
        recv(panels.at[0, :, g], pan_r.at[0, g])
        recv(panels.at[2, :, g], pan_r.at[2, g])

    @pl.loop(0, blk)
    def _(i):
        wide, tall = [], []
        for s in range(STEPS):
            k = kappa(s)
            inner = cols_ref[(row0 + i) * slabs + k]
            a = lefts[s, i]
            a_hi = a.astype(jnp.bfloat16)
            a_lo = (a - a_hi.astype(jnp.float32)).astype(jnp.bfloat16)
            tops, lows = [], []
            for g in range(groups):
                q = c * groups + g
                fits = cols_ref[(k * blk + inner) * slabs + q] == cols_ref[(row0 + i) * slabs + q]
                b = dens[inner, g] if s == 0 else panels[s - 1, inner, g]
                b = b * jnp.where(fits, 1, 0).astype(jnp.float32)
                b_hi = b.astype(jnp.bfloat16)
                tops.append(b_hi)
                lows.append((b - b_hi.astype(jnp.float32)).astype(jnp.bfloat16))
            top, low = jnp.concatenate(tops, axis=1), jnp.concatenate(lows, axis=1)
            wide += [a_hi, a_lo, a_hi]
            tall += [top, top, low]
        total = jnp.dot(jnp.concatenate(wide, axis=1), jnp.concatenate(tall, axis=0),
                        preferred_element_type=jnp.float32)
        for g in range(groups):
            out_ref[i, g] = total[:, g * bs:(g + 1) * bs]

    for g in range(groups):
        @pl.when(home != c)
        def _(g=g):
            to_relay(g).wait_send()

        @pl.when((home == c) & (c * groups + g != r))
        def _(g=g):
            last(g).wait_send()

        @pl.when(c * groups + g != r)
        def _(g=g):
            direct(g).wait_send()

        panel_two(g).wait_send()
        panel_sib(g).wait_send()
        pass_on(g, 0).wait_send()

    @pl.when(home == c)
    def _():
        @pl.loop(1, n_col)
        def _(d):
            for g in range(groups):
                forward((c + d) % n_col, g).wait_send()

    for s in range(STEPS):
        h = kappa(s) // groups
        for ch in range(CHUNKS):
            piece = lefts.at[s, pl.ds(ch * part, part)]

            @pl.when((c >= h) & (c + 1 < n_col))
            def _(s=s, ch=ch, piece=piece):
                left_from(s, ch, piece, 0).wait_send()

            @pl.when((c <= h) & (c > 0))
            def _(s=s, ch=ch, piece=piece):
                left_from(s, ch, piece, 1).wait_send()


def shards(n_row, n_col, x, block_cols, storage_map):
    blk, groups, bs = x.shape[0], x.shape[1], x.shape[2]
    cols = lax.all_gather(block_cols, "col", axis=1, tiled=True)
    cols = lax.all_gather(cols, "row", axis=0, tiled=True).reshape(-1)
    f32, dma = jnp.float32, pltpu.SemaphoreType.DMA
    vmem, smem = pl.BlockSpec(memory_space=pltpu.VMEM), pl.BlockSpec(memory_space=pltpu.SMEM)
    return pl.pallas_call(
        functools.partial(kernel, n_row, n_col),
        out_shape=jax.ShapeDtypeStruct(x.shape, f32),
        in_specs=[vmem, smem, smem],
        out_specs=vmem,
        scratch_shapes=[
            [pltpu.VMEM((blk, bs, bs), f32)] * groups,
            pltpu.VMEM((n_col, groups, blk // 2, bs, bs), f32),
            pltpu.VMEM((blk, groups, bs, bs), f32),
            pltpu.VMEM((STEPS - 1, blk, groups, bs, bs), f32),
            pltpu.VMEM((STEPS, blk, bs, bs), f32),
            dma((groups,)), dma((groups,)), dma((groups,)), dma((n_col, groups)), dma((n_col, groups)),
            dma((groups,)), dma((groups,)), dma,
            dma((3, groups)), dma((STEPS - 1, groups)), dma((STEPS,)),
            dma((STEPS, CHUNKS, 2)), dma((STEPS, CHUNKS)),
        ],
        compiler_params=pltpu.CompilerParams(
            collective_id=0, has_side_effects=True, vmem_limit_bytes=56 * 2**20),
    )(x, cols, storage_map.reshape(-1))


def solution(mesh):
    return jax.shard_map(
        functools.partial(shards, mesh.shape["row"], mesh.shape["col"]),
        mesh=mesh,
        in_specs=(P("row", "col", None, None), P("row", "col"), P("row", "col")),
        out_specs=P("row", "col", None, None),
        check_vma=False,
    )
```

time: 648 us -> 512 us (0.79)
  the two profiles are of different devices: /device:TPU:25 before, /device:TPU:7 now
where the time goes in v1:
time: 512 us
  Pallas kernels  485 us (95%)
  blocking collectives  19.9 us (4%)
  local copies, waits for them, and re-layouts  6.89 us (1%)
    pallas_call x1, Pallas kernels, shards(): pl.pallas_call(functools.partial(kernel, n_row, n_col), out_shape=jax.Sha...  485 us
    all_gather x1, blocking collectives, shards(): cols = lax.all_gather(cols, 'row', axis=0, tiled=True).reshape(-1)  10.6 us

profile of v1, /device:TPU:7, one launch (start us, length us, event | category | flops | bytes accessed | tf_op | source)
XLA Modules:
  0.0 512.0 jit_solution(8369074786144288482)
XLA Ops:
  0.0 9.4 %all-gather = s32[4,2,32]{2,1,0:T(2,128)S(1)} all-gather(s32[1,2,32]{2,1,0:T(2,128)} %bitcast.9), channel_id=1, replica_groups=mesh['row'=8,'col'=4] {'col'}, dimensions={0}, use_global_device_ids=true | all-gather | bytes 1280 | tf_op jit(solution)/shard_map/all_gather | solution.py:285
  9.4 0.8 copy.8
  10.1 0.6 reshape.7.map_ref
  10.8 10.6 %all-gather.1 = s32[8,32,8]{1,2,0:T(8,128)S(1)} all-gather(s32[1,32,8]{1,2,0:T(8,128)S(1)} %bitcast.8), channel_id=1, replica_groups=mesh['row'=8,'col'=4] {'row'}, dimensions={0}, use_global_device_ids=true | all-gather | bytes 9216 | tf_op jit(solution)/shard_map/all_gather | solution.py:286
  21.3 0.1 copy.7
  21.4 0.7 reshape.6.cols_ref
  22.1 485.2 %shard_map.37 = f32[32,2,128,128]{3,2,1,0:T(8,128)} custom-call(f32[32,2,128,128]{3,2,1,0:T(8,128)} %x_ref.1, s32[2048]{0:T(1024)} %reshape.6.cols_ref, s32[64]{0:T(128)} %reshape.7.map_ref), custom_call_target="tpu_custom_call" | custom-call | tf_op jit(solution)/shard_map/pallas_call | solution.py:289
  507.3 4.7 copy.10

commit v2 on v1

--- a/solution.py
+++ b/solution.py
@@ -13,13 +13,13 @@
 
 
 def kernel(n_row, n_col, x_ref, cols_ref, map_ref, out_ref, arr, relay, dens, panels, lefts,
-           dir_s, dir_r, rel_s, rel_r, fwd_s, last_s, last_r, self_s,
+           out_s, in_r, rel_r, fwd_s, self_s,
            pan_s, pan_r, own_s, left_s, left_r):
     blk, groups = x_ref.shape[0], x_ref.shape[1]
     bs = x_ref.shape[2]
-    slabs = n_row
     half = blk // 2
     part = blk // CHUNKS
+    bit = half // CHUNKS
     r, c = lax.axis_index("row"), lax.axis_index("col")
     home, slot = r // groups, r % groups
     core = r % 2
@@ -30,23 +30,17 @@
 
     barrier = pltpu.get_barrier_semaphore()
 
-    @pl.loop(1, n_col)
+    me, devices = r * n_col + c, n_row * n_col
+
+    @pl.loop(1, devices)
     def _(d):
-        pl.semaphore_signal(barrier, inc=1, device_id=(r, (c + d) % n_col), device_id_type=MESH)
-
-    @pl.loop(1, n_row)
-    def _(d):
-        pl.semaphore_signal(barrier, inc=1, device_id=((r + d) % n_row, c), device_id_type=MESH)
-
-    @pl.when(home != c)
-    def _():
-        for g in range(groups):
-            pl.semaphore_signal(barrier, inc=1, device_id=(c * groups + g, home), device_id_type=MESH)
-        pl.semaphore_wait(barrier, n_col + n_row - 2 + groups)
-
-    @pl.when(home == c)
-    def _():
-        pl.semaphore_wait(barrier, n_col + n_row - 2)
+        peer = (me + d) % devices
+        pl.semaphore_signal(barrier, inc=1, device_id=(peer // n_col, peer % n_col), device_id_type=MESH)
+
+    pl.semaphore_wait(barrier, devices - 1)
+
+    def recv(ref, sem):
+        pltpu.make_async_copy(ref, ref, sem).wait()
 
     lo, hi = pl.ds(0, half), pl.ds(half, half)
 
@@ -56,49 +50,69 @@
             def _(sl=sl):
                 copy(*place, arr[sl]).start()
 
-    def direct(g, tile=arr[0]):
-        return remote(x_ref.at[lo, g], tile.at[lo], dir_s.at[g], dir_r.at[slot], c * groups + g, home)
-
-    def to_relay(g):
-        return remote(x_ref.at[hi, g], relay.at[c, g], rel_s.at[g], rel_r.at[c, g], r, home)
-
-    def last(g, tile=arr[0]):
-        return remote(x_ref.at[hi, g], tile.at[hi], rel_s.at[g], last_r.at[slot], c * groups + g, home)
-
-    def forward(c2, g, tile=arr[0]):
-        return remote(relay.at[c2, g], tile.at[hi], fwd_s.at[c2, g], last_r.at[slot], c2 * groups + g, c)
+    chip = r // 2
+
+    def target(c2, g):
+        return c2 * groups + g
+
+    def bend(g, way):
+        aim = target(c, g) // 2
+        if way == 0:
+            return chip % 2 != aim % 2, (chip // 2 * 2 + aim % 2) * 2 + core
+        return chip // 2 != aim // 2, (aim // 2 * 2 + chip % 2) * 2 + core
+
+    part_of = (lo, hi)
+
+    def direct(g, way, tile=arr[0]):
+        return remote(x_ref.at[part_of[way], g], tile.at[part_of[way]], out_s.at[way, g], in_r.at[way, slot],
+                      target(c, g), home)
+
+    def to_relay(g, way, ch):
+        return remote(x_ref.at[pl.ds(way * half + ch * bit, bit), g], relay.at[chip, g, pl.ds(ch * bit, bit)],
+                      out_s.at[way, g], rel_r.at[chip, g, ch], bend(g, way)[1], c)
+
+    def passes(p, g, way):
+        aim = target(c, g) // 2
+        if way == 0:
+            return (p // 2 == chip // 2) & (p % 2 != chip % 2) & (aim % 2 == chip % 2)
+        return (p % 2 == chip % 2) & (p // 2 != chip // 2) & (aim // 2 == chip // 2)
+
+    def forward(p, g, way, ch, sl):
+        return remote(relay.at[p, g, pl.ds(ch * bit, bit)], arr[sl].at[pl.ds(way * half + ch * bit, bit)],
+                      fwd_s.at[p, g], in_r.at[way, sl], target(c, g), (2 * p + core) // groups)
 
     def own(g):
         return pltpu.make_async_copy(x_ref.at[:, g], arr[g], self_s)
 
     for g in range(groups):
-        @pl.when(home != c)
-        def _(g=g):
-            to_relay(g).start()
-
-        @pl.when((home == c) & (c * groups + g != r))
-        def _(g=g):
-            land(last, g)
-
-        @pl.when(c * groups + g != r)
-        def _(g=g):
-            land(direct, g)
-
-        @pl.when(c * groups + g == r)
+        for way in range(2):
+            turns = bend(g, way)[0]
+
+            @pl.when(turns & (target(c, g) != r))
+            def _(g=g, way=way):
+                for ch in range(CHUNKS):
+                    to_relay(g, way, ch).start()
+
+            @pl.when(jnp.logical_not(turns) & (target(c, g) != r))
+            def _(g=g, way=way):
+                land(direct, g, way)
+
+        @pl.when(target(c, g) == r)
         def _(g=g):
             own(g).start()
 
-    @pl.when(home == c)
-    def _():
-        @pl.loop(1, n_col)
-        def _(d):
-            c2 = (c + d) % n_col
+    for ch in range(CHUNKS):
+        @pl.loop(0, n_row // 2)
+        def _(p, ch=ch):
             for g in range(groups):
-                pltpu.make_async_copy(relay.at[c2, g], relay.at[c2, g], rel_r.at[c2, g]).wait()
-                land(forward, c2, g)
-
-    def recv(ref, sem):
-        pltpu.make_async_copy(ref, ref, sem).wait()
+                for way in range(2):
+                    @pl.when(passes(p, g, way))
+                    def _(g=g, way=way):
+                        recv(relay.at[p, g, pl.ds(ch * bit, bit)], rel_r.at[p, g, ch])
+                        for sl in range(groups):
+                            @pl.when((2 * p + core) % groups == sl)
+                            def _(sl=sl):
+                                forward(p, g, way, ch, sl).start()
 
     def panel_two(g):
         return remote(dens.at[:, g], panels.at[1, :, g], pan_s.at[0, g], pan_r.at[1, g], (r + n_row - 2) % n_row, c)
@@ -111,6 +125,9 @@
 
     def pass_on(g, s):
         return remote(panels.at[1, :, g], panels.at[s, :, g], pan_s.at[2, g], pan_r.at[s, g], r + 1 - 2 * core, c)
+
+    def col_of(k, i, q):
+        return cols_ref[((k * n_col + q // groups) * blk + i) * groups + q % groups]
 
     def kappa(s):
         return (r + s) % n_row
@@ -122,7 +139,6 @@
     def own_left(s):
         return pltpu.make_async_copy(dens.at[:, kappa(s) % groups], lefts.at[s], own_s.at[s])
 
-    row0 = r * blk
     for g in range(groups):
         q = c * groups + g
 
@@ -132,14 +148,14 @@
 
         @pl.when(q != r)
         def _(g=g):
-            recv(arr[g].at[lo], dir_r.at[g])
-            recv(arr[g].at[hi], last_r.at[g])
+            recv(arr[g].at[lo], in_r.at[0, g])
+            recv(arr[g].at[hi], in_r.at[1, g])
 
         on_diag = jnp.where(q == r, 1, 0)
 
         @pl.loop(0, blk)
         def _(i, g=g, q=q, on_diag=on_diag):
-            there = cols_ref[(row0 + i) * slabs + q]
+            there = col_of(r, i, q)
             here = map_ref[i * groups + g]
             same = on_diag * jnp.where(there == i, 1, 0)
             mine = here.astype(jnp.float32)
@@ -221,14 +237,14 @@
         wide, tall = [], []
         for s in range(STEPS):
             k = kappa(s)
-            inner = cols_ref[(row0 + i) * slabs + k]
+            inner = col_of(r, i, k)
             a = lefts[s, i]
             a_hi = a.astype(jnp.bfloat16)
             a_lo = (a - a_hi.astype(jnp.float32)).astype(jnp.bfloat16)
             tops, lows = [], []
             for g in range(groups):
                 q = c * groups + g
-                fits = cols_ref[(k * blk + inner) * slabs + q] == cols_ref[(row0 + i) * slabs + q]
+                fits = col_of(k, inner, q) == col_of(r, i, q)
                 b = dens[inner, g] if s == 0 else panels[s - 1, inner, g]
                 b = b * jnp.where(fits, 1, 0).astype(jnp.float32)
                 b_hi = b.astype(jnp.bfloat16)
@@ -243,28 +259,21 @@
             out_ref[i, g] = total[:, g * bs:(g + 1) * bs]
 
     for g in range(groups):
-        @pl.when(home != c)
-        def _(g=g):
-            to_relay(g).wait_send()
-
-        @pl.when((home == c) & (c * groups + g != r))
-        def _(g=g):
-            last(g).wait_send()
-
-        @pl.when(c * groups + g != r)
-        def _(g=g):
-            direct(g).wait_send()
+        @pl.when(target(c, g) != r)
+        def _(g=g):
+            for way in range(2):
+                direct(g, way).wait_send()
 
         panel_two(g).wait_send()
         panel_sib(g).wait_send()
         pass_on(g, 0).wait_send()
 
-    @pl.when(home == c)
-    def _():
-        @pl.loop(1, n_col)
-        def _(d):
-            for g in range(groups):
-                forward((c + d) % n_col, g).wait_send()
+    @pl.loop(0, n_row // 2)
+    def _(p):
+        for g in range(groups):
+            @pl.when(passes(p, g, 0) | passes(p, g, 1))
+            def _(g=g):
+                pltpu.make_async_copy(relay.at[p, g], relay.at[p, g], fwd_s.at[p, g]).wait()
 
     for s in range(STEPS):
         h = kappa(s) // groups
@@ -282,8 +291,7 @@
 
 def shards(n_row, n_col, x, block_cols, storage_map):
     blk, groups, bs = x.shape[0], x.shape[1], x.shape[2]
-    cols = lax.all_gather(block_cols, "col", axis=1, tiled=True)
-    cols = lax.all_gather(cols, "row", axis=0, tiled=True).reshape(-1)
+    cols = lax.all_gather(block_cols, ("row", "col"), axis=0, tiled=True).reshape(-1)
     f32, dma = jnp.float32, pltpu.SemaphoreType.DMA
     vmem, smem = pl.BlockSpec(memory_space=pltpu.VMEM), pl.BlockSpec(memory_space=pltpu.SMEM)
     return pl.pallas_call(
@@ -293,12 +301,11 @@
         out_specs=vmem,
         scratch_shapes=[
             [pltpu.VMEM((blk, bs, bs), f32)] * groups,
-            pltpu.VMEM((n_col, groups, blk // 2, bs, bs), f32),
+            pltpu.VMEM((n_row // 2, groups, blk // 2, bs, bs), f32),
             pltpu.VMEM((blk, groups, bs, bs), f32),
             pltpu.VMEM((STEPS - 1, blk, groups, bs, bs), f32),
             pltpu.VMEM((STEPS, blk, bs, bs), f32),
-            dma((groups,)), dma((groups,)), dma((groups,)), dma((n_col, groups)), dma((n_col, groups)),
-            dma((groups,)), dma((groups,)), dma,
+            dma((2, groups)), dma((2, groups)), dma((n_row // 2, groups, CHUNKS)), dma((n_row // 2, groups)), dma,
             dma((3, groups)), dma((STEPS - 1, groups)), dma((STEPS,)),
             dma((STEPS, CHUNKS, 2)), dma((STEPS, CHUNKS)),
         ],

time: 512 us -> 401 us (0.78)
  the two profiles are of different devices: /device:TPU:7 before, /device:TPU:25 now
where the time goes in v2:
time: 401 us
  Pallas kernels  338 us (84%)
  blocking collectives  55.9 us (14%)
  local copies, waits for them, and re-layouts  7.22 us (2%)
    pallas_call x1, Pallas kernels, shards(): pl.pallas_call(functools.partial(kernel, n_row, n_col), out_shape=jax.Sha...  338 us
    all_gather x1, blocking collectives, shards(): lax.all_gather(block_cols, ('row', 'col'), axis=0, tiled=True).reshape(-1)  55.9 us

profile of v2, /device:TPU:25, one launch (start us, length us, event | category | flops | bytes accessed | tf_op | source)
XLA Modules:
  0.0 401.3 jit_solution(14617083520459001431)
XLA Ops:
  0.0 0.8 copy.8
  0.8 0.6 reshape.7.map_ref
  1.4 55.9 %all-gather = s32[32,32,2]{1,2,0:T(2,128)S(1)} all-gather(s32[1,32,2]{1,2,0:T(2,128)} %bitcast.1), channel_id=1, replica_groups=mesh['row'=8,'col'=4] {'row','col'}, dimensions={0}, use_global_device_ids=true | all-gather | bytes 8448 | tf_op jit(solution)/shard_map/all_gather | solution.py:294
  57.3 0.3 copy.7
  57.6 0.9 reshape.6.cols_ref
  58.5 338.1 %shard_map.37 = f32[32,2,128,128]{3,2,1,0:T(8,128)} custom-call(f32[32,2,128,128]{3,2,1,0:T(8,128)} %x_ref.1, s32[2048]{0:T(1024)} %reshape.6.cols_ref, s32[64]{0:T(128)} %reshape.7.map_ref), custom_call_target="tpu_custom_call" | custom-call | tf_op jit(solution)/shard_map/pallas_call | solution.py:297
  396.6 4.7 %copy.10 = f32[32,2,128,128]{3,2,1,0:T(8,128)} copy(f32[32,2,128,128]{3,2,1,0:T(8,128)} %shard_map.37) | data formatting | bytes 8388608

commit v3 on v2

--- a/solution.py
+++ b/solution.py
@@ -127,7 +127,7 @@
         return remote(panels.at[1, :, g], panels.at[s, :, g], pan_s.at[2, g], pan_r.at[s, g], r + 1 - 2 * core, c)
 
     def col_of(k, i, q):
-        return cols_ref[((k * n_col + q // groups) * blk + i) * groups + q % groups]
+        return cols_ref[(k * blk + i) * n_col * groups + q]
 
     def kappa(s):
         return (r + s) % n_row
@@ -153,7 +153,7 @@
 
         on_diag = jnp.where(q == r, 1, 0)
 
-        @pl.loop(0, blk)
+        @pl.loop(0, blk, unroll=4)
         def _(i, g=g, q=q, on_diag=on_diag):
             there = col_of(r, i, q)
             here = map_ref[i * groups + g]
@@ -232,7 +232,7 @@
         recv(panels.at[0, :, g], pan_r.at[0, g])
         recv(panels.at[2, :, g], pan_r.at[2, g])
 
-    @pl.loop(0, blk)
+    @pl.loop(0, blk, unroll=2)
     def _(i):
         wide, tall = [], []
         for s in range(STEPS):
@@ -291,7 +291,8 @@
 
 def shards(n_row, n_col, x, block_cols, storage_map):
     blk, groups, bs = x.shape[0], x.shape[1], x.shape[2]
-    cols = lax.all_gather(block_cols, ("row", "col"), axis=0, tiled=True).reshape(-1)
+    cols = lax.all_gather(block_cols, "col", axis=1, tiled=True)
+    cols = lax.all_gather(cols, "row", axis=0, tiled=True).reshape(-1)
     f32, dma = jnp.float32, pltpu.SemaphoreType.DMA
     vmem, smem = pl.BlockSpec(memory_space=pltpu.VMEM), pl.BlockSpec(memory_space=pltpu.SMEM)
     return pl.pallas_call(

time: 401 us -> 348 us (0.87)
  blocking collectives: 55.9 us -> 17.1 us
  Pallas kernels: 338 us -> 324 us
    all_gather x1 -> x2, blocking collectives: 55.9 us -> 17.1 us  [the longest x1 11.3 us: shards(): cols = lax.all_gather(cols, 'row', axis=0, tiled=True).reshape(-1)]
    pallas_call x1, Pallas kernels: 338 us -> 324 us  [shards(): pl.pallas_call(functools.partial(kernel, n_row, n_col), out_shape=jax.Sha...]
where the time goes in v3:
time: 348 us
  Pallas kernels  324 us (93%)
  blocking collectives  17.1 us (5%)
  local copies, waits for them, and re-layouts  6.89 us (2%)
    pallas_call x1, Pallas kernels, shards(): pl.pallas_call(functools.partial(kernel, n_row, n_col), out_shape=jax.Sha...  324 us
    all_gather x1, blocking collectives, shards(): cols = lax.all_gather(cols, 'row', axis=0, tiled=True).reshape(-1)  11.3 us

profile of v3, /device:TPU:25, one launch (start us, length us, event | category | flops | bytes accessed | tf_op | source)
XLA Modules:
  0.0 348.1 jit_solution(730900982845061678)
XLA Ops:
  0.0 5.8 %all-gather = s32[4,2,32]{2,1,0:T(2,128)S(1)} all-gather(s32[1,2,32]{2,1,0:T(2,128)} %bitcast.9), channel_id=1, replica_groups=mesh['row'=8,'col'=4] {'col'}, dimensions={0}, use_global_device_ids=true | all-gather | bytes 1280 | tf_op jit(solution)/shard_map/all_gather | solution.py:294
  5.8 0.8 copy.8
  6.6 0.6 reshape.7.map_ref
  7.2 11.3 %all-gather.1 = s32[8,32,8]{1,2,0:T(8,128)S(1)} all-gather(s32[1,32,8]{1,2,0:T(8,128)S(1)} %bitcast.8), channel_id=1, replica_groups=mesh['row'=8,'col'=4] {'row'}, dimensions={0}, use_global_device_ids=true | all-gather | bytes 9216 | tf_op jit(solution)/shard_map/all_gather | solution.py:295
  18.5 0.1 copy.7
  18.6 0.7 reshape.6.cols_ref
  19.3 324.1 %shard_map.37 = f32[32,2,128,128]{3,2,1,0:T(8,128)} custom-call(f32[32,2,128,128]{3,2,1,0:T(8,128)} %x_ref.1, s32[2048]{0:T(1024)} %reshape.6.cols_ref, s32[64]{0:T(128)} %reshape.7.map_ref), custom_call_target="tpu_custom_call" | custom-call | tf_op jit(solution)/shard_map/pallas_call | solution.py:298
  343.4 4.7 %copy.10 = f32[32,2,128,128]{3,2,1,0:T(8,128)} copy(f32[32,2,128,128]{3,2,1,0:T(8,128)} %shard_map.37) | data formatting | bytes 8388608
